TPU v7x, 32 devices: a whole 2x2x4 slice. The times are simulated.
32 devices in a mesh: rows: 16 (over z, y, x), cols: 2 (over core).
Axes of the slice: x: 2, y: 2, z: 4, core: 2. Of those that a mesh axis runs over, the one named last changes fastest.
Arguments:
- embeddings: bfloat16 [32768, 384], P('rows')
- test_matrix: bfloat16 [32768, 64], P('rows'), may hold values from -6 to 6
- pair_list: int32 [128, 2], P(('rows', 'cols')), may hold values from -1 to 31, as said below
Outputs:
- orthonormal_basis: float32 [32768, 64], P(('rows', 'cols'))
- upper_factor: float32 [64, 64], replicated
Inputs may be any that keep to these rules, and one draw needn't show every extreme that they name: `pair_list`: device (r, c) holds 4 entries. Its live entries come first: pairs (i, j) with r * 2 <= i < (r + 1) * 2 and i <= j < min((r + 3) * 2, 32); each pair appears at most once over all devices; its other entries are -1 in both places. The device with c = 0 holds at least one live pair, the two devices of one r hold at most 4 together, and device (0, 0) holds exactly 4.
All inputs are finite; a program needn't handle non-finite values.
Results may differ from a plain program's by a relative error of at most 0.0053.
Values may be sent and summed in bfloat16 or wider, within the bound.
A program may use at most 64 MiB of HBM per device.

v0:
```python
import jax
import jax.numpy as jnp
from jax import lax
from jax.sharding import PartitionSpec as P

BLK = 1024


SHARPNESS = 6.0
EPSILON = 1e-06


def shifted(value, axis, steps):
    count = lax.axis_size(axis)
    initial, last = (max(0, -steps), min(count, count - steps))
    return lax.ppermute(value, axis, [(source, source + steps) for source in range(initial, last)])


def unit_rows(embeddings):
    widened = embeddings.astype(jnp.float32)
    inverse = lax.rsqrt(jnp.sum(widened * widened, axis=1, keepdims=True) + EPSILON)
    return (widened * inverse).astype(jnp.bfloat16)


def affinity(left_rows, right_rows):
    scores = lax.dot_general(
        left_rows, right_rows, (((1,), (1,)), ((), ())), preferred_element_type=jnp.float32
    )
    return jnp.exp(SHARPNESS * (scores - 1.0)).astype(jnp.bfloat16)


def mirror_product(affinity_tile, vectors):
    return lax.dot_general(
        affinity_tile, vectors, (((0,), (0,)), ((), ())), preferred_element_type=jnp.float32
    )


def block_at(stacked, index):
    return lax.dynamic_index_in_dim(stacked, index, 0, keepdims=False)


def add_block(stacked, index, term):
    return lax.dynamic_update_index_in_dim(stacked, block_at(stacked, index) + term, index, 0)


def count_live(pair_rows):
    return jnp.sum((pair_rows[:, 0] >= 0).astype(jnp.int32))


def orthonormal(sketch_rows, rows_total):
    gram_matrix = lax.dot_general(
        sketch_rows,
        sketch_rows,
        (((0,), (0,)), ((), ())),
        precision=lax.Precision.HIGHEST,
        preferred_element_type=jnp.float32,
    )
    gram_matrix = lax.psum(gram_matrix, ("rows", "cols")) / rows_total
    lower_factor = jnp.linalg.cholesky(gram_matrix)
    solved = lax.linalg.triangular_solve(
        lower_factor, sketch_rows, left_side=False, lower=True, transpose_a=True
    )
    return (solved, lower_factor.T)


def affinity_pass(window_units, own_vectors, my_pairs, base_block):
    blocks_dev = own_vectors.shape[0]
    ahead_vectors = [shifted(own_vectors, "rows", -offset) for offset in (1, 2)]
    window_vectors = jnp.concatenate([own_vectors] + ahead_vectors, axis=0)
    initial = jnp.zeros(window_vectors.shape, jnp.float32)

    def pair_step(slot_index, accumulated):
        entry = my_pairs[slot_index]
        first_block = entry[0] - base_block
        second_block = entry[1] - base_block
        affinity_tile = affinity(
            block_at(window_units, first_block), block_at(window_units, second_block)
        )
        forward = jnp.dot(
            affinity_tile,
            block_at(window_vectors, second_block),
            preferred_element_type=jnp.float32,
        )
        accumulated = add_block(accumulated, first_block, forward)
        mirrored = first_block != second_block

        def add_mirror(current):
            return add_block(
                current,
                second_block,
                mirror_product(affinity_tile, block_at(window_vectors, first_block)),
            )

        return lax.cond(mirrored, add_mirror, lambda unchanged: unchanged, accumulated)

    accumulated = lax.fori_loop(0, count_live(my_pairs), pair_step, initial)
    own_blocks = accumulated[:blocks_dev]
    for offset in (1, 2):
        own_blocks = own_blocks + shifted(
            accumulated[offset * blocks_dev : (offset + 1) * blocks_dev], "rows", offset
        )
    flattened = own_blocks.reshape(-1, own_blocks.shape[2])
    return lax.psum_scatter(flattened, "cols", scatter_dimension=0, tiled=True)


def local(embeddings, test_matrix, pair_list):
    rows_dev = embeddings.shape[0]
    blocks_dev = rows_dev // BLK
    columns = test_matrix.shape[1]
    base_block = lax.axis_index("rows") * blocks_dev
    rows_total = rows_dev * lax.axis_size("rows")
    normed = unit_rows(embeddings).reshape(blocks_dev, BLK, embeddings.shape[1])
    ahead_units = [shifted(normed, "rows", -offset) for offset in (1, 2)]
    window_units = jnp.concatenate([normed] + ahead_units, axis=0)
    sketch_rows = affinity_pass(
        window_units, test_matrix.reshape(blocks_dev, BLK, columns), pair_list, base_block
    )
    panel_rows, _ = orthonormal(sketch_rows, rows_total)
    panel_whole = lax.all_gather(panel_rows.astype(jnp.bfloat16), "cols", axis=0, tiled=True)
    image_rows = affinity_pass(
        window_units, panel_whole.reshape(blocks_dev, BLK, columns), pair_list, base_block
    )
    return orthonormal(image_rows, rows_total)


def solution(mesh):
    in_specs = (P("rows", None), P("rows", None), P(("rows", "cols"), None))
    out_specs = (P(("rows", "cols"), None), P())
    return jax.shard_map(local, mesh=mesh, in_specs=in_specs, out_specs=out_specs, check_vma=False)
```

profile of v0, /device:TPU:0, one launch (start us, length us, event | category | flops | bytes accessed | tf_op | source)
XLA Modules:
  0.0 439.5 jit_solution(7014263315393171880)
XLA Ops:
  15.7 44.3 %collective-permute-done.2 = bf16[2,1024,64]{2,1,0:T(8,128)(2,1)S(1)} collective-permute-done((bf16[2,1024,64]{2,1,0:T(8,128)(2,1)S(1)}, bf16[2,1024,64]{2,1,0:T(8,128)(2,1)S(1)}, u32[]{:S(2)}, u32[]{:S(2)}) %collective-permute-start.2) | collective-permute-done | bytes 262176 | tf_op jit(solution)/shard_map/ppermute | solution.py:16
  60.0 3.1 collective-permute-done.3
  64.6 3.8 pad_maximum_fusion
  69.8 44.9 %while.24 = (s32[]{:T(128)}, f32[6,1024,64]{1,2,0:T(8,128)}, s32[]{:T(128)}, s32[4,2]{0,1:T(2,128)S(1)}, s32[]{:T(128)}, /*index=5*/bf16[6,1024,384]{2,1,0:T(8,1...) while((s32[]{:T(128)}, f32[6,1024,64]{1,2,0:T(8,128)}, ...), condition=%wide.region_5.6_spmd, body=%wide.region_2.5_spmd.sunk | while | flops 1077018624 | bytes 10486193 | solution.py:96
  72.3 2.7 exponential_convert_fusion.4
  76.0 2.4 fusion.78
  78.5 3.1 conditional.4
  79.5 2.2 fusion.2
  84.2 2.7 exponential_convert_fusion.4
  87.9 2.4 fusion.78
  90.3 3.2 conditional.4
  91.3 2.2 fusion.2
  96.1 2.7 exponential_convert_fusion.4
  99.8 2.4 fusion.78
  104.8 2.7 exponential_convert_fusion.4
  108.5 2.4 fusion.78
  110.9 3.1 conditional.4
  111.9 2.2 fusion.2
  116.0 25.8 %collective-permute-start.4 = (f32[2,1024,64]{1,2,0:T(8,128)S(1)}, f32[2,1024,64]{1,2,0:T(8,128)S(1)}, u32[]{:S(2)}, u32[]{:S(2)}) collective-permute-start(f32[2,1024,64]{1,2,0:T(8,128)S(1)} %get-tuple-element.272), channel_id=1, source_target_pairs={{0,2},{2,4},{4,6},{6,8},{8,10},{10,12},{12,14},{14,16},{16,18},{18... | collective-permute-start | bytes 1572872 | tf_op jit(solution)/shard_map/ppermute | solution.py:16
  141.8 47.1 %collective-permute-start.5 = (f32[2,1024,64]{1,2,0:T(8,128)S(1)}, f32[2,1024,64]{1,2,0:T(8,128)S(1)}, u32[]{:S(2)}, u32[]{:S(2)}) collective-permute-start(f32[2,1024,64]{1,2,0:T(8,128)S(1)} %get-tuple-element.273), channel_id=1, source_target_pairs={{0,4},{2,6},{4,8},{6,10},{8,12},{10,14},{12,16},{14,18},{16,20},{1... | collective-permute-start | bytes 1572872 | tf_op jit(solution)/shard_map/ppermute | solution.py:16
  189.0 11.2 %collective-permute-done.5 = f32[2,1024,64]{1,2,0:T(8,128)S(1)} collective-permute-done((f32[2,1024,64]{1,2,0:T(8,128)S(1)}, f32[2,1024,64]{1,2,0:T(8,128)S(1)}, u32[]{:S(2)}, u32[]{:S(2)}) %collective-permute-start.5) | collective-permute-done | bytes 524320 | tf_op jit(solution)/shard_map/ppermute | solution.py:16
  202.3 7.2 %reduce-scatter.3.cloned.1.call-done = f32[1024,64]{0,1:T(8,128)} async-done(((f32[2048,64]{0,1:T(8,128)}), f32[1024,64]{0,1:T(8,128)}) %reduce-scatter.3.cloned.1.call-update) | async-done | bytes 262160 | tf_op jit(solution)/shard_map/reduce_scatter | solution.py:103
  211.0 40.7 %psum.14 = f32[64,64]{0,1:T(8,128)S(1)} all-reduce(f32[64,64]{0,1:T(8,128)S(1)} %fusion.49), channel_id=1, replica_groups=mesh['rows'=16,'cols'=2] {'rows','cols'}, use_global_device_ids=true, to_apply=%region_7.8 | all-reduce | flops 4096 | bytes 32768 | tf_op jit(solution)/shard_map/psum | solution.py:58
  251.8 5.8 %cholesky.44 = f32[64,64]{1,0:T(8,128)S(1)} custom-call(f32[64,64]{1,0:T(8,128)S(1)} %fusion.39), custom_call_target="Cholesky" | custom-call | tf_op jit(solution)/shard_map/jit(cholesky)/cholesky | solution.py:59
  258.9 4.9 %custom-call.6 = f32[1,64,64]{1,2,0:T(8,128)S(1)} custom-call(f32[1,64,64]{2,1,0:T(8,128)S(1)} %fusion.35), custom_call_target="InvertDiagBlocksLowerTriangular" | custom-call | tf_op jit(solution)/shard_map/triangular_solve/custom-call.0 | solution.py:60
  270.1 13.8 %collective-permute-done.6 = bf16[2,1024,64]{2,1,0:T(8,128)(2,1)S(1)} collective-permute-done((bf16[2,1024,64]{2,1,0:T(8,128)(2,1)S(1)}, bf16[2,1024,64]{2,1,0:T(8,128)(2,1)S(1)}, u32[]{:S(2)}, u32[]{:S(2)}) %collective-permute-start.6) | collective-permute-done | bytes 262176 | tf_op jit(solution)/shard_map/ppermute | solution.py:16
  283.9 3.1 collective-permute-done.7
  289.8 44.9 %while.25 = (s32[]{:T(128)}, f32[6,1024,64]{1,2,0:T(8,128)}, s32[]{:T(128)}, s32[4,2]{0,1:T(2,128)S(1)}, s32[]{:T(128)}, /*index=5*/bf16[6,1024,384]{2,1,0:T(8,1...) while((s32[]{:T(128)}, f32[6,1024,64]{1,2,0:T(8,128)}, ...), condition=%wide.region_13.16_spmd, body=%wide.region_10.0_spmd.sunk | while | flops 1077018624 | bytes 10486193 | solution.py:96
  292.4 2.7 exponential_convert_fusion.5
  296.1 2.4 fusion.84
  298.5 3.1 conditional.5
  299.5 2.2 fusion.18
  304.2 2.7 exponential_convert_fusion.5
  307.9 2.4 fusion.84
  310.4 3.2 conditional.5
  311.4 2.2 fusion.18
  316.1 2.7 exponential_convert_fusion.5
  319.8 2.4 fusion.84
  324.8 2.7 exponential_convert_fusion.5
  328.5 2.4 fusion.84
  331.0 3.1 conditional.5
  332.0 2.2 fusion.18
  337.4 18.6 %collective-permute-start.9 = (f32[2,1024,64]{1,2,0:T(8,128)S(1)}, f32[2,1024,64]{1,2,0:T(8,128)S(1)}, u32[]{:S(2)}, u32[]{:S(2)}) collective-permute-start(f32[2,1024,64]{1,2,0:T(8,128)S(1)} %get-tuple-element.271), channel_id=1, source_target_pairs={{0,4},{2,6},{4,8},{6,10},{8,12},{10,14},{12,16},{14,18},{16,20},{1... | collective-permute-start | bytes 1572872 | tf_op jit(solution)/shard_map/ppermute | solution.py:16
  356.0 11.0 %collective-permute-done.9 = f32[2,1024,64]{1,2,0:T(8,128)S(1)} collective-permute-done((f32[2,1024,64]{1,2,0:T(8,128)S(1)}, f32[2,1024,64]{1,2,0:T(8,128)S(1)}, u32[]{:S(2)}, u32[]{:S(2)}) %collective-permute-start.9) | collective-permute-done | bytes 524320 | tf_op jit(solution)/shard_map/ppermute | solution.py:16
  369.0 6.6 %reduce-scatter.5.cloned.1.call-done = f32[1024,64]{0,1:T(8,128)} async-done(((f32[2048,64]{0,1:T(8,128)}), f32[1024,64]{0,1:T(8,128)}) %reduce-scatter.5.cloned.1.call-update) | async-done | bytes 262160 | tf_op jit(solution)/shard_map/reduce_scatter | solution.py:103
  377.0 40.7 %psum.15 = f32[64,64]{0,1:T(8,128)S(1)} all-reduce(f32[64,64]{0,1:T(8,128)S(1)} %fusion.50), channel_id=1, replica_groups=mesh['rows'=16,'cols'=2] {'rows','cols'}, use_global_device_ids=true, to_apply=%region_15.18 | all-reduce | flops 4096 | bytes 32768 | tf_op jit(solution)/shard_map/psum | solution.py:58
  417.8 5.8 %cholesky.55 = f32[64,64]{1,0:T(8,128)S(1)} custom-call(f32[64,64]{1,0:T(8,128)S(1)} %fusion.37), custom_call_target="Cholesky" | custom-call | tf_op jit(solution)/shard_map/jit(cholesky)/cholesky | solution.py:59
  425.0 4.9 %custom-call.7 = f32[1,64,64]{1,2,0:T(8,128)S(1)} custom-call(f32[1,64,64]{2,1,0:T(8,128)S(1)} %get-tuple-element.275), custom_call_target="InvertDiagBlocksLowerTriangular" | custom-call | tf_op jit(solution)/shard_map/triangular_solve/custom-call.0 | solution.py:60
  (87 shorter events, 55.6 us)
Async XLA Ops:
  7.2 2.0 copy-start
  7.2 202.3 %reduce-scatter.3.cloned.1.call-start = ((), (), s32[]{:S(2)}) async-start(), calls=%async_computation.2 | async-start | bytes 786432 | tf_op jit(solution)/shard_map/reduce_scatter | solution.py:103
  9.1 3.0 copy-start.1
  9.2 5.9 %copy-start.2 = (s32[4,2]{0,1:T(2,128)S(1)}, s32[4,2]{0,1:T(2,128)}, u32[]{:S(2)}) copy-start(s32[4,2]{0,1:T(2,128)} %param.16) | copy-start | bytes 100
  9.5 55.1 %collective-permute-start = (bf16[2,1024,384]{2,1,0:T(8,128)(2,1)S(1)}, bf16[2,1024,384]{2,1,0:T(8,128)(2,1)}, u32[]{:S(2)}, u32[]{:S(2)}) collective-permute-start(bf16[2,1024,384]{2,1,0:T(8,128)(2,1)S(1)} %bitcast.145), channel_id=1, source_target_pairs={{2,0},{4,2},{6,4},{8,6},{10,8},{12,10},{14,12},{16,14},{18,16},{20... | collective-permute-start | bytes 4718600 | tf_op jit(solution)/shard_map/ppermute | solution.py:16
  10.8 53.8 %collective-permute-start.1 = (bf16[2,1024,384]{2,1,0:T(8,128)(2,1)S(1)}, bf16[2,1024,384]{2,1,0:T(8,128)(2,1)}, u32[]{:S(2)}, u32[]{:S(2)}) collective-permute-start(bf16[2,1024,384]{2,1,0:T(8,128)(2,1)S(1)} %bitcast.146), channel_id=1, source_target_pairs={{4,0},{6,2},{8,4},{10,6},{12,8},{14,10},{16,12},{18,14},{20,16},{2... | collective-permute-start | bytes 4718600 | tf_op jit(solution)/shard_map/ppermute | solution.py:16
  12.4 47.6 %collective-permute-start.2 = (bf16[2,1024,64]{2,1,0:T(8,128)(2,1)S(1)}, bf16[2,1024,64]{2,1,0:T(8,128)(2,1)S(1)}, u32[]{:S(2)}, u32[]{:S(2)}) collective-permute-start(bf16[2,1024,64]{2,1,0:T(8,128)(2,1)S(1)} %bitcast.150), channel_id=1, source_target_pairs={{2,0},{4,2},{6,4},{8,6},{10,8},{12,10},{14,12},{16,14},{18,16},{20... | collective-permute-start | bytes 786440 | tf_op jit(solution)/shard_map/ppermute | solution.py:16
  13.7 49.4 %collective-permute-start.3 = (bf16[2,1024,64]{2,1,0:T(8,128)(2,1)S(1)}, bf16[2,1024,64]{2,1,0:T(8,128)(2,1)S(1)}, u32[]{:S(2)}, u32[]{:S(2)}) collective-permute-start(bf16[2,1024,64]{2,1,0:T(8,128)(2,1)S(1)} %bitcast.151), channel_id=1, source_target_pairs={{4,0},{6,2},{8,4},{10,6},{12,8},{14,10},{16,12},{18,14},{20,16},{2... | collective-permute-start | bytes 786440 | tf_op jit(solution)/shard_map/ppermute | solution.py:16
  116.0 73.0 %collective-permute-start.4 = (f32[2,1024,64]{1,2,0:T(8,128)S(1)}, f32[2,1024,64]{1,2,0:T(8,128)S(1)}, u32[]{:S(2)}, u32[]{:S(2)}) collective-permute-start(f32[2,1024,64]{1,2,0:T(8,128)S(1)} %get-tuple-element.272), channel_id=1, source_target_pairs={{0,2},{2,4},{4,6},{6,8},{8,10},{10,12},{12,14},{14,16},{16,18},{18... | collective-permute-start | bytes 1572872 | tf_op jit(solution)/shard_map/ppermute | solution.py:16
  141.8 58.4 %collective-permute-start.5 = (f32[2,1024,64]{1,2,0:T(8,128)S(1)}, f32[2,1024,64]{1,2,0:T(8,128)S(1)}, u32[]{:S(2)}, u32[]{:S(2)}) collective-permute-start(f32[2,1024,64]{1,2,0:T(8,128)S(1)} %get-tuple-element.273), channel_id=1, source_target_pairs={{0,4},{2,6},{4,8},{6,10},{8,12},{10,14},{12,16},{14,18},{16,20},{1... | collective-permute-start | bytes 1572872 | tf_op jit(solution)/shard_map/ppermute | solution.py:16
  202.2 173.4 %reduce-scatter.5.cloned.1.call-start = ((), (), s32[]{:S(2)}) async-start(), calls=%async_computation.3 | async-start | bytes 786432 | tf_op jit(solution)/shard_map/reduce_scatter | solution.py:103
  267.5 16.4 %collective-permute-start.6 = (bf16[2,1024,64]{2,1,0:T(8,128)(2,1)S(1)}, bf16[2,1024,64]{2,1,0:T(8,128)(2,1)S(1)}, u32[]{:S(2)}, u32[]{:S(2)}) collective-permute-start(bf16[2,1024,64]{2,1,0:T(8,128)(2,1)S(1)} %bitcast.153), channel_id=1, source_target_pairs={{2,0},{4,2},{6,4},{8,6},{10,8},{12,10},{14,12},{16,14},{18,16},{20... | collective-permute-start | bytes 786440 | tf_op jit(solution)/shard_map/ppermute | solution.py:16
  268.8 18.2 %collective-permute-start.7 = (bf16[2,1024,64]{2,1,0:T(8,128)(2,1)S(1)}, bf16[2,1024,64]{2,1,0:T(8,128)(2,1)S(1)}, u32[]{:S(2)}, u32[]{:S(2)}) collective-permute-start(bf16[2,1024,64]{2,1,0:T(8,128)(2,1)S(1)} %bitcast.154), channel_id=1, source_target_pairs={{4,0},{6,2},{8,4},{10,6},{12,8},{14,10},{16,12},{18,14},{20,16},{2... | collective-permute-start | bytes 786440 | tf_op jit(solution)/shard_map/ppermute | solution.py:16
  336.1 19.9 %collective-permute-start.8 = (f32[2,1024,64]{1,2,0:T(8,128)S(1)}, f32[2,1024,64]{1,2,0:T(8,128)S(1)}, u32[]{:S(2)}, u32[]{:S(2)}) collective-permute-start(f32[2,1024,64]{1,2,0:T(8,128)S(1)} %get-tuple-element.270), channel_id=1, source_target_pairs={{0,2},{2,4},{4,6},{6,8},{8,10},{10,12},{12,14},{14,16},{16,18},{18... | collective-permute-start | bytes 1572872 | tf_op jit(solution)/shard_map/ppermute | solution.py:16
  337.4 29.6 %collective-permute-start.9 = (f32[2,1024,64]{1,2,0:T(8,128)S(1)}, f32[2,1024,64]{1,2,0:T(8,128)S(1)}, u32[]{:S(2)}, u32[]{:S(2)}) collective-permute-start(f32[2,1024,64]{1,2,0:T(8,128)S(1)} %get-tuple-element.271), channel_id=1, source_target_pairs={{0,4},{2,6},{4,8},{6,10},{8,12},{10,14},{12,16},{14,18},{16,20},{1... | collective-permute-start | bytes 1572872 | tf_op jit(solution)/shard_map/ppermute | solution.py:16
Sparse Core Ops, SparseCore 0:
  202.4 7.0 reduce-scatter.2
  369.2 6.4 reduce-scatter.4
where the time goes:
time: 442 us; the launch traced here: 440 us
  starting transfers between devices  101 us (23%)
  waiting for transfers between devices  100 us (23%)
  blocking collectives  83.4 us (19%)
  matrix products  60.5 us (14%)
  other arithmetic  36.2 us (8%)
  local copies, waits for them, and re-layouts  27.2 us (6%)
  loops' own time  16.8 us (4%)
  between operations  14.4 us (3%)
    ppermute x10, starting transfers between devices, shifted(): lax.ppermute(value, axis, [(source, source + steps) for source in range(i...  101 us
    ppermute x10, waiting for transfers between devices, shifted(): lax.ppermute(value, axis, [(source, source + steps) for source in range(i...  86.6 us
    psum x2, blocking collectives, orthonormal(): gram_matrix = lax.psum(gram_matrix, ('rows', 'cols')) / rows_total  81.4 us
    dot_general x8, matrix products, affinity(): lax.dot_general(left_rows, right_rows, (((1,), (1,)), ((), ())), preferre...  21.7 us
    dot_general x8, matrix products, pair_step(): jnp.dot(affinity_tile, block_at(window_vectors, second_block), preferred_...  19.6 us
    another operation x2, loops' own time, affinity_pass(): accumulated = lax.fori_loop(0, count_live(my_pairs), pair_step, initial)  16.7 us
    reduce_scatter x2, waiting for transfers between devices, affinity_pass(): return lax.psum_scatter(flattened, 'cols', scatter_dimension=0, tiled=True)  13.8 us
    dynamic_slice x14, local copies, waits for them, and re-layouts, block_at(): return lax.dynamic_index_in_dim(stacked, index, 0, keepdims=False)  13.6 us
  transfers between devices with their start and end apart: 12, of which 8 were waited for; matrix products, arithmetic and copies ran while one was open for 1% of the time, Pallas kernels for 0%

commit v1 on v0

v1 whole, which is shorter than its diff:
```python
import functools

import jax
import jax.numpy as jnp
from jax import lax
from jax.experimental import pallas as pl
from jax.experimental.pallas import tpu as pltpu
from jax.sharding import PartitionSpec as P

BLK = 1024
SHARPNESS = 6.0
EPSILON = 1e-06
QUAD = 4
PIECES = 4
PIECE = BLK // PIECES
TILE = 256
MESH = pl.DeviceIdType.MESH
F32 = jnp.float32
BF16 = jnp.bfloat16


def dot_nt(left, right, precision=None):
    return lax.dot_general(
        left, right, (((1,), (1,)), ((), ())), precision=precision, preferred_element_type=F32
    )


def unit_rows(rows):
    widened = rows.astype(F32)
    inverse = lax.rsqrt(jnp.sum(widened * widened, axis=1, keepdims=True) + EPSILON)
    return (widened * inverse).astype(BF16)


def factor_and_inverse(gram):
    size = gram.shape[0]
    row_at = lax.broadcasted_iota(jnp.int32, (size, size), 0)
    lane_at = lax.broadcasted_iota(jnp.int32, (size, size), 1)
    augmented = jnp.concatenate([gram, (row_at == lane_at).astype(F32)], axis=1)
    parts = [augmented[8 * t : 8 * t + 8] for t in range(size // 8)]
    within = lax.broadcasted_iota(jnp.int32, (8, 1), 0)
    done = []
    for k in range(size):
        t, s = divmod(k, 8)
        row = parts[t][s : s + 1, :]
        pivot = row[:, k : k + 1]
        done.append(row * lax.rsqrt(pivot))
        scaled = row * (1.0 / pivot)
        for u in range(t, size // 8):
            column = parts[u][:, k : k + 1]
            if u == t:
                column = jnp.where(within > s, column, 0.0)
            parts[u] = parts[u] - column * scaled
    whole = jnp.concatenate(done, axis=0)
    upper = jnp.where(row_at <= lane_at, whole[:, :size], 0.0)
    return upper, whole[:, size:]


def kernel(
    count,
    pair_ref,
    emb_ref,
    test_ref,
    basis_ref,
    upper_ref,
    win,
    vec,
    aff,
    fwd,
    mir,
    sib_out,
    sib_in,
    mir_out,
    mir_in,
    gram_out,
    gram_in,
    unit_send,
    unit_recv,
    pass_send,
    pass_recv,
    vec_send,
    vec_recv,
    sib_send,
    sib_recv,
    mir_send,
    mir_recv,
    gram_send,
    gram_recv,
):
    r = lax.axis_index("rows")
    c = lax.axis_index("cols")
    other = 1 - c
    rounds = []
    stride = QUAD
    while stride < count:
        size = min(QUAD, count // stride)
        rounds.append((stride, size))
        stride *= size

    def first_partner(d):
        at = (c * QUAD + r % QUAD + d) % (2 * QUAD)
        return at, ((r // QUAD) * QUAD + at % QUAD, at // QUAD)

    def later_partner(stride, size, d):
        at = (r // stride + d) % size
        span = stride * size
        return at, ((r // span) * span + at * stride + r % stride, c)

    def remote(src, dst, send, recv, device):
        return pltpu.make_async_remote_copy(
            src_ref=src, dst_ref=dst, send_sem=send, recv_sem=recv,
            device_id=device, device_id_type=MESH,
        )

    barrier = pltpu.get_barrier_semaphore()

    def greet(device):
        pl.semaphore_signal(barrier, inc=1, device_id=device, device_id_type=MESH)

    for d in range(1, 2 * QUAD):
        greet(first_partner(d)[1])
    for stride, size in rounds:
        for d in range(1, size):
            greet(later_partner(stride, size, d)[1])
    peers = 2 * QUAD - 1 + sum(size - 1 for _, size in rounds)
    for k in (1, 2):
        below = jnp.logical_and(r % QUAD < k, r >= k)
        above = jnp.logical_and(r % QUAD + k >= QUAD, r + k < count)
        peers = peers + below.astype(jnp.int32) + above.astype(jnp.int32)

        @pl.when(below)
        def _(k=k):
            greet((r - k, c))

        @pl.when(above)
        def _(k=k):
            greet((r + k, c))

    def normalise(block):
        for q in range(PIECES):
            rows = emb_ref[pl.ds(pl.multiple_of(block * BLK + q * PIECE, PIECE), PIECE), :]
            win[block, pl.ds(q * PIECE, PIECE), :] = unit_rows(rows)

    normalise(c)
    pl.semaphore_wait(barrier, peers)

    def piece(block, q):
        return win.at[block, pl.ds(q * PIECE, PIECE), :]

    def unit_copy(k, q, device, src_block):
        return remote(
            piece(src_block, q), piece(2 * k + c, q),
            unit_send.at[k - 1, q], unit_recv.at[k - 1, q], device,
        )

    def unit_pass(k, q):
        return remote(
            piece(2 * k + c, q), piece(2 * k + c, q),
            pass_send.at[k - 1, q], pass_recv.at[k - 1, q], (r, other),
        )

    def unit_pass_in(k, q):
        return remote(
            piece(2 * k + other, q), piece(2 * k + other, q),
            pass_send.at[k - 1, q], pass_recv.at[k - 1, q], (r, other),
        )

    even = r % 2 == 0
    for q in range(PIECES):
        @pl.when(r >= 2)
        def _(q=q):
            unit_copy(2, q, (r - 2, c), c).start()

        @pl.when(r % 2 == 1)
        def _(q=q):
            unit_copy(1, q, (r - 1, c), c).start()

    def vec_copy(p, k, device):
        return remote(
            vec.at[p, c], vec.at[p, 2 * k + c], vec_send.at[p, k], vec_recv.at[p, k], device
        )

    def vec_pass(p, k):
        return remote(
            vec.at[p, 2 * k + c], vec.at[p, 2 * k + c],
            vec_send.at[p, 2 + k if k else 0], vec_recv.at[p, 2 + k if k else 0], (r, other),
        )

    def vec_pass_in(p, k):
        return remote(
            vec.at[p, 2 * k + other], vec.at[p, 2 * k + other],
            vec_send.at[p, 2 + k if k else 0], vec_recv.at[p, 2 + k if k else 0], (r, other),
        )

    def vec_start(p):
        for k in (2, 1):
            @pl.when(r >= k)
            def _(k=k):
                vec_copy(p, k, (r - k, c)).start()

    def vec_finish(p):
        for k in (1, 2):
            @pl.when(r + k < count)
            def _(k=k):
                vec_copy(p, k, (r, other)).wait_recv()
                vec_pass(p, k).start()
        for k in (1, 2):
            @pl.when(r + k < count)
            def _(k=k):
                vec_pass_in(p, k).wait_recv()

    for b in (0, 1):
        vec[0, b] = test_ref[b * BLK : (b + 1) * BLK, :].astype(F32).T.astype(BF16)
    vec_start(0)
    normalise(other)

    for k in (1, 2):
        @pl.when(r + k >= count)
        def _(k=k):
            for b in (2 * k, 2 * k + 1):
                win[b] = jnp.zeros(win.shape[1:], BF16)
                for p in (0, 1):
                    vec[p, b] = jnp.zeros(vec.shape[2:], BF16)

        @pl.when(r < k)
        def _(k=k):
            for p in (0, 1):
                mir_in[p, k - 1] = jnp.zeros(mir_in.shape[2:], BF16)

    for q in range(PIECES):
        @pl.when(r + 2 < count)
        def _(q=q):
            unit_copy(2, q, (r, other), c).wait_recv()
            unit_pass(2, q).start()

            @pl.when(even)
            def _():
                unit_copy(1, q, (r + 1, c), 4 + c).start()

        @pl.when(r + 1 < count)
        def _(q=q):
            unit_copy(1, q, (r, other), c).wait_recv()
            unit_pass(1, q).start()
    vec_finish(0)
    for q in range(PIECES):
        for k in (1, 2):
            @pl.when(r + k < count)
            def _(k=k, q=q):
                unit_pass_in(k, q).wait_recv()

    live = jnp.int32(0)
    for slot in range(4):
        live = live + (pair_ref[slot, 0] >= 0).astype(jnp.int32)
    firsts, seconds, lives = [], [], []
    for s in (0, 1):
        rank = 2 * c + s
        entry = jnp.clip(jnp.where(rank < live, rank, 4 + rank - live), 0, 7)
        first = pair_ref[entry, 0]
        second = pair_ref[entry, 1]
        alive = first >= 0
        firsts.append(jnp.clip(first - 2 * r, 0, 1))
        seconds.append(jnp.clip(second - 2 * r, 0, 5))
        lives.append(alive)

    def multiply(p):
        for s in (0, 1):
            i, j = firsts[s], seconds[s]
            mirrored = None
            for t in range(BLK // TILE):
                span = pl.ds(t * TILE, TILE)
                if p == 0:
                    scores = dot_nt(win[i, span, :], win[j])
                    tile = jnp.exp(SHARPNESS * (scores - 1.0)).astype(BF16)
                    aff[s, span, :] = tile
                else:
                    tile = aff[s, span, :]
                fwd[s, :, span] = dot_nt(vec[p, j], tile)
                term = jnp.dot(vec[p, i, :, span], tile, preferred_element_type=F32)
                mirrored = term if mirrored is None else mirrored + term
            mir[s] = mirrored

    def weight(flag):
        return flag.astype(F32)

    def block_sum(k, side):
        total = None
        for s in (0, 1):
            here = 2 * k + side
            off = jnp.logical_and(lives[s], firsts[s] != seconds[s])
            term = weight(jnp.logical_and(off, seconds[s] == here)) * mir[s]
            if k == 0:
                term = term + weight(jnp.logical_and(lives[s], firsts[s] == here)) * fwd[s]
            total = term if total is None else total + term
        return total

    def sib_copy(p, k):
        return remote(
            sib_out.at[k], sib_in.at[p, k], sib_send.at[p, k], sib_recv.at[p, k], (r, other)
        )

    def mir_copy(p, k, device):
        return remote(
            mir_out.at[p, k - 1], mir_in.at[p, k - 1],
            mir_send.at[p, k - 1], mir_recv.at[p, k - 1], device,
        )

    def collect(p):
        for k in (2, 1, 0):
            sib_out[k] = block_sum(k, other)
            sib_copy(p, k).start()
        for k in (2, 1):
            mine = block_sum(k, c)
            sib_copy(p, k).wait_recv()
            mir_out[p, k - 1] = (mine + sib_in[p, k]).astype(BF16)

            @pl.when(r + k < count)
            def _(k=k):
                mir_copy(p, k, (r + k, c)).start()
        total = block_sum(0, c)
        sib_copy(p, 0).wait_recv()
        total = total + sib_in[p, 0]
        for k in (1, 2):
            @pl.when(r >= k)
            def _(k=k):
                mir_copy(p, k, (r, other)).wait_recv()
        for k in (1, 2):
            total = total + mir_in[p, k - 1].astype(F32)
        for k in (0, 1, 2):
            sib_copy(p, k).wait_send()
        return total

    def gram_copy(p, n, d, to, at_slot):
        return remote(
            gram_out.at[p, n], gram_in.at[p, n, at_slot],
            gram_send.at[p, n, d], gram_recv.at[p, n, at_slot], to,
        )

    def sum_over_devices(p, value):
        steps = [(2 * QUAD, first_partner, c * QUAD + r % QUAD)]
        for stride, size in rounds:
            steps.append(
                (size, functools.partial(later_partner, stride, size), (r // stride) % size)
            )
        for n, (size, partner, me) in enumerate(steps):
            gram_out[p, n] = value
            gram_in[p, n, me] = value
            for d in range(1, size):
                gram_copy(p, n, d, partner(d)[1], me).start()
            for d in range(1, size):
                at, device = partner(d)
                gram_copy(p, n, d, device, at).wait_recv()
            value = gram_in[p, n, 0]
            for m in range(1, size):
                value = value + gram_in[p, n, m]
            for d in range(1, size):
                gram_copy(p, n, d, partner(d)[1], me).wait_send()
        return value

    rows_total = count * emb_ref.shape[0]

    def orthonormal(p, total):
        gram = dot_nt(total, total, lax.Precision.HIGHEST)
        gram = sum_over_devices(p, gram) * (1.0 / rows_total)
        upper, inverse = factor_and_inverse(gram)
        solved = jnp.dot(
            inverse, total, precision=lax.Precision.HIGHEST, preferred_element_type=F32
        )
        return solved, upper

    multiply(0)
    panel, _ = orthonormal(0, collect(0))
    vec[1, c] = panel.astype(BF16)
    vec_pass(1, 0).start()
    vec_start(1)
    vec_finish(1)
    vec_pass_in(1, 0).wait_recv()
    multiply(1)
    basis, upper = orthonormal(1, collect(1))
    upper_ref[...] = upper
    basis_ref[...] = basis.T

    vec_pass(1, 0).wait_send()
    for k in (1, 2):
        @pl.when(r >= k)
        def _(k=k):
            for p in (0, 1):
                vec_copy(p, k, (r - k, c)).wait_send()

        @pl.when(r + k < count)
        def _(k=k):
            for p in (0, 1):
                vec_pass(p, k).wait_send()
                mir_copy(p, k, (r + k, c)).wait_send()
            for q in range(PIECES):
                unit_pass(k, q).wait_send()
    for q in range(PIECES):
        @pl.when(r >= 2)
        def _(q=q):
            unit_copy(2, q, (r - 2, c), c).wait_send()

        @pl.when(r % 2 == 1)
        def _(q=q):
            unit_copy(1, q, (r - 1, c), c).wait_send()

        @pl.when(jnp.logical_and(even, r + 2 < count))
        def _(q=q):
            unit_copy(1, q, (r + 1, c), 4 + c).wait_send()


def local(count, embeddings, test_matrix, pair_list):
    columns = test_matrix.shape[1]
    width = embeddings.shape[1]
    blocks = embeddings.shape[0] // BLK
    window = 3 * blocks
    group_pairs = lax.all_gather(pair_list, "cols", axis=0, tiled=True)
    steps = 1
    stride = QUAD
    while stride < count:
        stride *= min(QUAD, count // stride)
        steps += 1
    vmem = pl.BlockSpec(memory_space=pltpu.VMEM)
    dma = pltpu.SemaphoreType.DMA
    return pl.pallas_call(
        functools.partial(kernel, count),
        out_shape=(
            jax.ShapeDtypeStruct((BLK, columns), F32),
            jax.ShapeDtypeStruct((columns, columns), F32),
        ),
        in_specs=[pl.BlockSpec(memory_space=pltpu.SMEM), vmem, vmem],
        out_specs=(vmem, vmem),
        scratch_shapes=[
            pltpu.VMEM((window, BLK, width), BF16),
            pltpu.VMEM((2, window, columns, BLK), BF16),
            pltpu.VMEM((2, BLK, BLK), BF16),
            pltpu.VMEM((2, columns, BLK), F32),
            pltpu.VMEM((2, columns, BLK), F32),
            pltpu.VMEM((3, columns, BLK), F32),
            pltpu.VMEM((2, 3, columns, BLK), F32),
            pltpu.VMEM((2, 2, columns, BLK), BF16),
            pltpu.VMEM((2, 2, columns, BLK), BF16),
            pltpu.VMEM((2, steps, columns, columns), F32),
            pltpu.VMEM((2, steps, 2 * QUAD, columns, columns), F32),
            dma((2, PIECES)),
            dma((2, PIECES)),
            dma((2, PIECES)),
            dma((2, PIECES)),
            dma((2, 5)),
            dma((2, 5)),
            dma((2, 3)),
            dma((2, 3)),
            dma((2, 2)),
            dma((2, 2)),
            dma((2, steps, 2 * QUAD)),
            dma((2, steps, 2 * QUAD)),
        ],
        compiler_params=pltpu.CompilerParams(
            collective_id=0, has_side_effects=True, vmem_limit_bytes=48 * 1024 * 1024
        ),
    )(group_pairs, embeddings, test_matrix)


def solution(mesh):
    in_specs = (P("rows", None), P("rows", None), P(("rows", "cols"), None))
    out_specs = (P(("rows", "cols"), None), P())
    return jax.shard_map(
        functools.partial(local, mesh.shape["rows"]),
        mesh=mesh, in_specs=in_specs, out_specs=out_specs, check_vma=False,
    )
```

time: 442 us -> 102 us (0.23)
  starting transfers between devices: 101 us -> 0 us
  waiting for transfers between devices: 100 us -> 0 us
  Pallas kernels: 0 us -> 95.1 us
  blocking collectives: 83.4 us -> 2.13 us
  matrix products: 60.5 us -> 0 us
  other arithmetic: 36.2 us -> 0 us
  local copies, waits for them, and re-layouts: 27.2 us -> 4.23 us
  loops' own time: 16.8 us -> 0 us
  between operations: 14.4 us -> 0.65 us
    ppermute x10 -> x0, starting transfers between devices: 101 us -> none  [shifted(): lax.ppermute(value, axis, [(source, source + steps) for source in range(i...]
    pallas_call x0 -> x1, Pallas kernels: none -> 95.1 us  [local(): pl.pallas_call(functools.partial(kernel, count), out_shape=(jax.ShapeDtyp...]
    ppermute x10 -> x0, waiting for transfers between devices: 86.6 us -> none  [shifted(): lax.ppermute(value, axis, [(source, source + steps) for source in range(i...]
    psum x2 -> x0, blocking collectives: 81.4 us -> none  [orthonormal(): gram_matrix = lax.psum(gram_matrix, ('rows', 'cols')) / rows_total]
    dot_general x24 -> x0, matrix products: 57.1 us -> none  [the longest x8 21.7 us: affinity(): lax.dot_general(left_rows, right_rows, (((1,), (1,)), ((), ())), preferre...]
    another operation x9 -> x0, other arithmetic: 23.5 us -> none  [the longest x6 13 us: orthonormal(): lower_factor = jnp.linalg.cholesky(gram_matrix)]
    another operation x10 -> x0, loops' own time: 16.8 us -> none  [the longest x2 16.7 us: affinity_pass(): accumulated = lax.fori_loop(0, count_live(my_pairs), pair_step, initial)]
    dynamic_slice x22 -> x0, local copies, waits for them, and re-layouts: 14.2 us -> none  [the longest x14 13.6 us: block_at(): return lax.dynamic_index_in_dim(stacked, index, 0, keepdims=False)]
  transfers between devices with their start and end apart: 12 -> 0, of which waited for: 8 -> 0; matrix products, arithmetic and copies ran while one was open for 1% -> 0% of each run, Pallas kernels for 0% -> 0%
where the time goes in v1:
time: 102 us
  Pallas kernels  95.1 us (93%)
  local copies, waits for them, and re-layouts  4.23 us (4%)
  blocking collectives  2.13 us (2%)
    pallas_call x1, Pallas kernels, local(): pl.pallas_call(functools.partial(kernel, count), out_shape=(jax.ShapeDtyp...  95.1 us
    unnamed x5, local copies, waits for them, and re-layouts  3.34 us
    all_gather x1, blocking collectives, local(): group_pairs = lax.all_gather(pair_list, 'cols', axis=0, tiled=True)  2.13 us

profile of v1, /device:TPU:0, one launch (start us, length us, event | category | flops | bytes accessed | tf_op | source)
XLA Modules:
  0.0 102.2 jit_solution(1263179084305132076)
XLA Ops:
  0.6 2.1 %all-gather = s32[2,4,2]{1,2,0:T(2,128)S(1)} all-gather(s32[1,4,2]{1,2,0:T(2,128)} %bitcast.3), channel_id=1, replica_groups=mesh['rows'=16,'cols'=2] {'cols'}, dimensions={0}, use_global_device_ids=true | all-gather | bytes 96 | tf_op jit(solution)/shard_map/all_gather | solution.py:414
  2.8 0.1 copy.13
  2.9 1.2 %copy.11.test_ref = bf16[2048,64]{1,0:T(8,128)(2,1)S(1)} copy(bf16[2048,64]{0,1:T(8,128)(2,1)} %param.4) | data formatting | bytes 524288 | tf_op args[1]
  4.1 0.0 copy-start
  4.1 1.4 %copy-done = bf16[2048,384]{1,0:T(8,128)(2,1)S(1)} copy-done((bf16[2048,384]{1,0:T(8,128)(2,1)S(1)}, bf16[2048,384]{1,0:T(8,128)(2,1)}, u32[]{:S(2)}) %copy-start) | copy-done | bytes 1572888
  5.5 95.1 %shard_map.50 = (f32[1024,64]{1,0:T(8,128)S(1)}, f32[64,64]{1,0:T(8,128)S(1)}) custom-call(s32[8,2]{1,0:T(8,128)S(1)} %bitcast.2, bf16[2048,384]{1,0:T(8,128)(2,1)S(1)} %copy-done, bf16[2048,64]{1,0:T(8,128)(2,1)S(1)} %copy.11.test_ref), custom_call_target="tpu_custom_call" | custom-call | tf_op jit(solution)/shard_map/pallas_call | solution.py:422
  100.6 0.9 copy.12
  101.5 0.6 copy.16
Async XLA Ops:
  4.1 1.4 %copy-start = (bf16[2048,384]{1,0:T(8,128)(2,1)S(1)}, bf16[2048,384]{1,0:T(8,128)(2,1)}, u32[]{:S(2)}) copy-start(bf16[2048,384]{1,0:T(8,128)(2,1)} %emb_ref.1) | copy-start | bytes 4718596

commit v2 on v1

--- a/solution.py
+++ b/solution.py
@@ -13,7 +13,9 @@
 QUAD = 4
 PIECES = 4
 PIECE = BLK // PIECES
-TILE = 256
+SUBS = 2
+SUB = PIECE // SUBS
+PIVOTS = 4
 MESH = pl.DeviceIdType.MESH
 F32 = jnp.float32
 BF16 = jnp.bfloat16
@@ -39,17 +41,28 @@
     parts = [augmented[8 * t : 8 * t + 8] for t in range(size // 8)]
     within = lax.broadcasted_iota(jnp.int32, (8, 1), 0)
     done = []
-    for k in range(size):
+    for k in range(0, size, PIVOTS):
         t, s = divmod(k, 8)
-        row = parts[t][s : s + 1, :]
-        pivot = row[:, k : k + 1]
-        done.append(row * lax.rsqrt(pivot))
-        scaled = row * (1.0 / pivot)
-        for u in range(t, size // 8):
-            column = parts[u][:, k : k + 1]
-            if u == t:
-                column = jnp.where(within > s, column, 0.0)
-            parts[u] = parts[u] - column * scaled
+        rows = [parts[t][s + q : s + q + 1, :] for q in range(PIVOTS)]
+        columns = [
+            [jnp.broadcast_to(parts[u][:, k + q : k + q + 1], (8, 2 * size)) for u in range(t, size // 8)]
+            for q in range(PIVOTS)
+        ]
+        for q in range(PIVOTS):
+            at = s + q
+            pivot = columns[q][0][at : at + 1, :]
+            inverse = 1.0 / pivot
+            done.append(rows[q] * lax.rsqrt(pivot))
+            columns[q][0] = jnp.where(within > at, columns[q][0], 0.0)
+            for later in range(q + 1, PIVOTS):
+                ratio = columns[later][0][at : at + 1, :] * inverse
+                rows[later] = rows[later] - ratio * rows[q]
+                columns[later] = [
+                    mine - ratio * first for mine, first in zip(columns[later], columns[q])
+                ]
+            scaled = rows[q] * inverse
+            for u in range(t, size // 8):
+                parts[u] = parts[u] - columns[q][u - t] * scaled
     whole = jnp.concatenate(done, axis=0)
     upper = jnp.where(row_at <= lane_at, whole[:, :size], 0.0)
     return upper, whole[:, size:]
@@ -62,8 +75,17 @@
     test_ref,
     basis_ref,
     upper_ref,
-    win,
-    vec,
+    raw,
+    own,
+    win_0,
+    win_1,
+    win_2,
+    win_3,
+    vown_0,
+    vown_1,
+    vwin_0,
+    vwin_1,
+    pair_in,
     aff,
     fwd,
     mir,
@@ -73,6 +95,8 @@
     mir_in,
     gram_out,
     gram_in,
+    load_sem,
+    pair_sem,
     unit_send,
     unit_recv,
     pass_send,
@@ -86,6 +110,9 @@
     gram_send,
     gram_recv,
 ):
+    win = (win_0, win_1, win_2, win_3)
+    vown = (vown_0, vown_1)
+    vwin = (vwin_0, vwin_1)
     r = lax.axis_index("rows")
     c = lax.axis_index("cols")
     other = 1 - c
@@ -110,6 +137,15 @@
             src_ref=src, dst_ref=dst, send_sem=send, recv_sem=recv,
             device_id=device, device_id_type=MESH,
         )
+
+    def load(side, q):
+        block = c if side == 0 else other
+        span = pl.ds(pl.multiple_of(block * BLK + q * PIECE, PIECE), PIECE)
+        return pltpu.make_async_copy(emb_ref.at[span, :], raw.at[span, :], load_sem.at[side, q])
+
+    for side in (0, 1):
+        for q in range(PIECES):
+            load(side, q).start()
 
     barrier = pltpu.get_barrier_semaphore()
 
@@ -135,60 +171,70 @@
         def _(k=k):
             greet((r + k, c))
 
-    def normalise(block):
-        for q in range(PIECES):
-            rows = emb_ref[pl.ds(pl.multiple_of(block * BLK + q * PIECE, PIECE), PIECE), :]
-            win[block, pl.ds(q * PIECE, PIECE), :] = unit_rows(rows)
-
-    normalise(c)
+    def normalise(side, q):
+        block = c if side == 0 else other
+        load(side, q).wait()
+        span = pl.ds(pl.multiple_of(block * BLK + q * PIECE, PIECE), PIECE)
+        rows = unit_rows(raw[span, :])
+        own[block, pl.ds(q * PIECE, PIECE), :] = rows
+        win[q][block] = rows
+
+    for b in (0, 1):
+        block = test_ref[:, b * BLK : (b + 1) * BLK]
+        vown[0][b] = block
+        vwin[0][b] = block
+    normalise(0, 0)
     pl.semaphore_wait(barrier, peers)
 
-    def piece(block, q):
-        return win.at[block, pl.ds(q * PIECE, PIECE), :]
-
-    def unit_copy(k, q, device, src_block):
-        return remote(
-            piece(src_block, q), piece(2 * k + c, q),
-            unit_send.at[k - 1, q], unit_recv.at[k - 1, q], device,
-        )
-
-    def unit_pass(k, q):
-        return remote(
-            piece(2 * k + c, q), piece(2 * k + c, q),
-            pass_send.at[k - 1, q], pass_recv.at[k - 1, q], (r, other),
-        )
-
-    def unit_pass_in(k, q):
-        return remote(
-            piece(2 * k + other, q), piece(2 * k + other, q),
-            pass_send.at[k - 1, q], pass_recv.at[k - 1, q], (r, other),
+    pair_copy = remote(pair_ref, pair_in, pair_sem.at[0], pair_sem.at[1], (r, other))
+    pair_copy.start()
+
+    def piece(block, q, h):
+        return win[q].at[block, pl.ds(h * SUB, SUB), :]
+
+    def unit_copy(k, q, h, device, src_block):
+        n = q * SUBS + h
+        return remote(
+            piece(src_block, q, h), piece(2 * k + c, q, h),
+            unit_send.at[k - 1, n], unit_recv.at[k - 1, n], device,
+        )
+
+    def unit_pass(k, q, h):
+        n = q * SUBS + h
+        return remote(
+            piece(2 * k + c, q, h), piece(2 * k + c, q, h),
+            pass_send.at[k - 1, n], pass_recv.at[k - 1, n], (r, other),
+        )
+
+    def unit_pass_in(k, q, h):
+        n = q * SUBS + h
+        return remote(
+            piece(2 * k + other, q, h), piece(2 * k + other, q, h),
+            pass_send.at[k - 1, n], pass_recv.at[k - 1, n], (r, other),
         )
 
     even = r % 2 == 0
-    for q in range(PIECES):
-        @pl.when(r >= 2)
-        def _(q=q):
-            unit_copy(2, q, (r - 2, c), c).start()
-
-        @pl.when(r % 2 == 1)
-        def _(q=q):
-            unit_copy(1, q, (r - 1, c), c).start()
 
     def vec_copy(p, k, device):
         return remote(
-            vec.at[p, c], vec.at[p, 2 * k + c], vec_send.at[p, k], vec_recv.at[p, k], device
+            vown[p].at[c], vwin[p].at[2 * k + c], vec_send.at[p, k], vec_recv.at[p, k], device
         )
 
     def vec_pass(p, k):
         return remote(
-            vec.at[p, 2 * k + c], vec.at[p, 2 * k + c],
-            vec_send.at[p, 2 + k if k else 0], vec_recv.at[p, 2 + k if k else 0], (r, other),
+            vwin[p].at[2 * k + c], vwin[p].at[2 * k + c],
+            vec_send.at[p, 2 + k], vec_recv.at[p, 2 + k], (r, other),
         )
 
     def vec_pass_in(p, k):
         return remote(
-            vec.at[p, 2 * k + other], vec.at[p, 2 * k + other],
-            vec_send.at[p, 2 + k if k else 0], vec_recv.at[p, 2 + k if k else 0], (r, other),
+            vwin[p].at[2 * k + other], vwin[p].at[2 * k + other],
+            vec_send.at[p, 2 + k], vec_recv.at[p, 2 + k], (r, other),
+        )
+
+    def panel_copy(block):
+        return remote(
+            vown[1].at[block], vown[1].at[block], vec_send.at[1, 0], vec_recv.at[1, 0], (r, other)
         )
 
     def vec_start(p):
@@ -208,75 +254,97 @@
             def _(k=k):
                 vec_pass_in(p, k).wait_recv()
 
-    for b in (0, 1):
-        vec[0, b] = test_ref[b * BLK : (b + 1) * BLK, :].astype(F32).T.astype(BF16)
     vec_start(0)
-    normalise(other)
+    for q in range(PIECES):
+        if q:
+            normalise(0, q)
+        for h in range(SUBS):
+            @pl.when(r >= 2)
+            def _(q=q, h=h):
+                unit_copy(2, q, h, (r - 2, c), c).start()
+
+            @pl.when(r % 2 == 1)
+            def _(q=q, h=h):
+                unit_copy(1, q, h, (r - 1, c), c).start()
+    for q in range(PIECES):
+        normalise(1, q)
 
     for k in (1, 2):
         @pl.when(r + k >= count)
         def _(k=k):
             for b in (2 * k, 2 * k + 1):
-                win[b] = jnp.zeros(win.shape[1:], BF16)
+                for q in range(PIECES):
+                    win[q][b] = jnp.zeros(win[q].shape[1:], BF16)
                 for p in (0, 1):
-                    vec[p, b] = jnp.zeros(vec.shape[2:], BF16)
+                    vwin[p][b] = jnp.zeros(vwin[p].shape[1:], BF16)
 
         @pl.when(r < k)
         def _(k=k):
             for p in (0, 1):
                 mir_in[p, k - 1] = jnp.zeros(mir_in.shape[2:], BF16)
 
-    for q in range(PIECES):
-        @pl.when(r + 2 < count)
-        def _(q=q):
-            unit_copy(2, q, (r, other), c).wait_recv()
-            unit_pass(2, q).start()
-
-            @pl.when(even)
-            def _():
-                unit_copy(1, q, (r + 1, c), 4 + c).start()
-
-        @pl.when(r + 1 < count)
-        def _(q=q):
-            unit_copy(1, q, (r, other), c).wait_recv()
-            unit_pass(1, q).start()
-    vec_finish(0)
-    for q in range(PIECES):
-        for k in (1, 2):
-            @pl.when(r + k < count)
-            def _(k=k, q=q):
-                unit_pass_in(k, q).wait_recv()
-
+    pair_copy.wait()
+    on_first = c == 0
     live = jnp.int32(0)
     for slot in range(4):
-        live = live + (pair_ref[slot, 0] >= 0).astype(jnp.int32)
+        head = jnp.where(on_first, pair_ref[slot, 0], pair_in[slot, 0])
+        live = live + (head >= 0).astype(jnp.int32)
     firsts, seconds, lives = [], [], []
     for s in (0, 1):
         rank = 2 * c + s
-        entry = jnp.clip(jnp.where(rank < live, rank, 4 + rank - live), 0, 7)
-        first = pair_ref[entry, 0]
-        second = pair_ref[entry, 1]
-        alive = first >= 0
-        firsts.append(jnp.clip(first - 2 * r, 0, 1))
-        seconds.append(jnp.clip(second - 2 * r, 0, 5))
-        lives.append(alive)
-
-    def multiply(p):
+        in_head = rank < live
+        rest = jnp.clip(rank - live, 0, 3)
+        ends = []
+        for side in (0, 1):
+            head = jnp.where(on_first, pair_ref[rank, side], pair_in[rank, side])
+            tail = jnp.where(on_first, pair_in[rest, side], pair_ref[rest, side])
+            ends.append(jnp.where(in_head, head, tail))
+        firsts.append(jnp.clip(ends[0] - 2 * r, 0, 1))
+        seconds.append(jnp.clip(ends[1] - 2 * r, 0, 5))
+        lives.append(ends[0] >= 0)
+
+    def tile_of(s, q):
+        scores = dot_nt(own[firsts[s]], win[q][seconds[s]])
+        tile = jnp.exp(SHARPNESS * (scores - 1.0)).astype(BF16)
+        aff[s, q] = tile
+        return tile
+
+    def mirror(p, s, q, tile):
+        mir[s, :, pl.ds(q * PIECE, PIECE)] = jnp.dot(
+            vown[p][firsts[s]], tile, preferred_element_type=F32
+        )
+
+    def forward(p, s, q, tile):
+        return dot_nt(vwin[p][seconds[s], :, pl.ds(q * PIECE, PIECE)], tile)
+
+    for q in range(PIECES):
+        for h in range(SUBS):
+            @pl.when(r + 2 < count)
+            def _(q=q, h=h):
+                unit_copy(2, q, h, (r, other), c).wait_recv()
+
+                @pl.when(even)
+                def _():
+                    unit_copy(1, q, h, (r + 1, c), 4 + c).start()
+
+                unit_pass(2, q, h).start()
+
+            @pl.when(r + 1 < count)
+            def _(q=q, h=h):
+                unit_copy(1, q, h, (r, other), c).wait_recv()
+                unit_pass(1, q, h).start()
+        if q == 0:
+            vec_finish(0)
+        for h in range(SUBS):
+            for k in (1, 2):
+                @pl.when(r + k < count)
+                def _(k=k, q=q, h=h):
+                    unit_pass_in(k, q, h).wait_recv()
         for s in (0, 1):
-            i, j = firsts[s], seconds[s]
-            mirrored = None
-            for t in range(BLK // TILE):
-                span = pl.ds(t * TILE, TILE)
-                if p == 0:
-                    scores = dot_nt(win[i, span, :], win[j])
-                    tile = jnp.exp(SHARPNESS * (scores - 1.0)).astype(BF16)
-                    aff[s, span, :] = tile
-                else:
-                    tile = aff[s, span, :]
-                fwd[s, :, span] = dot_nt(vec[p, j], tile)
-                term = jnp.dot(vec[p, i, :, span], tile, preferred_element_type=F32)
-                mirrored = term if mirrored is None else mirrored + term
-            mir[s] = mirrored
+            tile = tile_of(s, q)
+            mirror(0, s, q, tile)
+            term = forward(0, s, q, tile)
+            fwd[s] = fwd[s] + term if q else term
 
     def weight(flag):
         return flag.astype(F32)
@@ -303,8 +371,8 @@
             mir_send.at[p, k - 1], mir_recv.at[p, k - 1], device,
         )
 
-    def collect(p):
-        for k in (2, 1, 0):
+    def send_mirrors(p):
+        for k in (2, 1):
             sib_out[k] = block_sum(k, other)
             sib_copy(p, k).start()
         for k in (2, 1):
@@ -315,6 +383,10 @@
             @pl.when(r + k < count)
             def _(k=k):
                 mir_copy(p, k, (r + k, c)).start()
+
+    def collect(p):
+        sib_out[0] = block_sum(0, other)
+        sib_copy(p, 0).start()
         total = block_sum(0, c)
         sib_copy(p, 0).wait_recv()
         total = total + sib_in[p, 0]
@@ -366,19 +438,30 @@
         )
         return solved, upper
 
-    multiply(0)
+    send_mirrors(0)
     panel, _ = orthonormal(0, collect(0))
-    vec[1, c] = panel.astype(BF16)
-    vec_pass(1, 0).start()
+    panel = panel.astype(BF16)
+    vown[1][c] = panel
+    panel_copy(c).start()
     vec_start(1)
+    vwin[1][c] = panel
+    panel_copy(other).wait_recv()
+    for s in (0, 1):
+        for q in range(PIECES):
+            mirror(1, s, q, aff[s, q])
+    send_mirrors(1)
+    vwin[1][other] = vown[1][other]
     vec_finish(1)
-    vec_pass_in(1, 0).wait_recv()
-    multiply(1)
+    for s in (0, 1):
+        total = forward(1, s, 0, aff[s, 0])
+        for q in range(1, PIECES):
+            total = total + forward(1, s, q, aff[s, q])
+        fwd[s] = total
     basis, upper = orthonormal(1, collect(1))
     upper_ref[...] = upper
-    basis_ref[...] = basis.T
-
-    vec_pass(1, 0).wait_send()
+    basis_ref[...] = basis
+
+    panel_copy(c).wait_send()
     for k in (1, 2):
         @pl.when(r >= k)
         def _(k=k):
@@ -391,19 +474,21 @@
                 vec_pass(p, k).wait_send()
                 mir_copy(p, k, (r + k, c)).wait_send()
             for q in range(PIECES):
-                unit_pass(k, q).wait_send()
+                for h in range(SUBS):
+                    unit_pass(k, q, h).wait_send()
     for q in range(PIECES):
-        @pl.when(r >= 2)
-        def _(q=q):
-            unit_copy(2, q, (r - 2, c), c).wait_send()
-
-        @pl.when(r % 2 == 1)
-        def _(q=q):
-            unit_copy(1, q, (r - 1, c), c).wait_send()
-
-        @pl.when(jnp.logical_and(even, r + 2 < count))
-        def _(q=q):
-            unit_copy(1, q, (r + 1, c), 4 + c).wait_send()
+        for h in range(SUBS):
+            @pl.when(r >= 2)
+            def _(q=q, h=h):
+                unit_copy(2, q, h, (r - 2, c), c).wait_send()
+
+            @pl.when(r % 2 == 1)
+            def _(q=q, h=h):
+                unit_copy(1, q, h, (r - 1, c), c).wait_send()
+
+            @pl.when(jnp.logical_and(even, r + 2 < count))
+            def _(q=q, h=h):
+                unit_copy(1, q, h, (r + 1, c), 4 + c).wait_send()
 
 
 def local(count, embeddings, test_matrix, pair_list):
@@ -411,7 +496,6 @@
     width = embeddings.shape[1]
     blocks = embeddings.shape[0] // BLK
     window = 3 * blocks
-    group_pairs = lax.all_gather(pair_list, "cols", axis=0, tiled=True)
     steps = 1
     stride = QUAD
     while stride < count:
@@ -419,18 +503,22 @@
         steps += 1
     vmem = pl.BlockSpec(memory_space=pltpu.VMEM)
     dma = pltpu.SemaphoreType.DMA
-    return pl.pallas_call(
+    basis, upper = pl.pallas_call(
         functools.partial(kernel, count),
         out_shape=(
-            jax.ShapeDtypeStruct((BLK, columns), F32),
+            jax.ShapeDtypeStruct((columns, BLK), F32),
             jax.ShapeDtypeStruct((columns, columns), F32),
         ),
-        in_specs=[pl.BlockSpec(memory_space=pltpu.SMEM), vmem, vmem],
+        in_specs=[pl.BlockSpec(memory_space=pltpu.SMEM), pl.BlockSpec(memory_space=pl.ANY), vmem],
         out_specs=(vmem, vmem),
         scratch_shapes=[
-            pltpu.VMEM((window, BLK, width), BF16),
-            pltpu.VMEM((2, window, columns, BLK), BF16),
-            pltpu.VMEM((2, BLK, BLK), BF16),
+            pltpu.VMEM((blocks * BLK, width), BF16),
+            pltpu.VMEM((blocks, BLK, width), BF16),
+            *[pltpu.VMEM((window, PIECE, width), BF16)] * PIECES,
+            *[pltpu.VMEM((blocks, columns, BLK), BF16)] * 2,
+            *[pltpu.VMEM((window, columns, BLK), BF16)] * 2,
+            pltpu.SMEM(pair_list.shape, jnp.int32),
+            pltpu.VMEM((2, PIECES, BLK, PIECE), BF16),
             pltpu.VMEM((2, columns, BLK), F32),
             pltpu.VMEM((2, columns, BLK), F32),
             pltpu.VMEM((3, columns, BLK), F32),
@@ -440,9 +528,11 @@
             pltpu.VMEM((2, steps, columns, columns), F32),
             pltpu.VMEM((2, steps, 2 * QUAD, columns, columns), F32),
             dma((2, PIECES)),
-            dma((2, PIECES)),
-            dma((2, PIECES)),
-            dma((2, PIECES)),
+            dma((2,)),
+            dma((2, PIECES * SUBS)),
+            dma((2, PIECES * SUBS)),
+            dma((2, PIECES * SUBS)),
+            dma((2, PIECES * SUBS)),
             dma((2, 5)),
             dma((2, 5)),
             dma((2, 3)),
@@ -455,7 +545,8 @@
         compiler_params=pltpu.CompilerParams(
             collective_id=0, has_side_effects=True, vmem_limit_bytes=48 * 1024 * 1024
         ),
-    )(group_pairs, embeddings, test_matrix)
+    )(pair_list, embeddings, test_matrix.T)
+    return basis.T, upper
 
 
 def solution(mesh):

time: 102 us -> 94.3 us (0.925)
  Pallas kernels: 95.1 us -> 89.1 us
  blocking collectives: 2.13 us -> 0 us
    pallas_call x1, Pallas kernels: 95.1 us -> 89.1 us  [local(): pl.pallas_call(functools.partial(kernel, count), out_shape=(jax.ShapeDtyp...]
    all_gather x1 -> x0, blocking collectives: 2.13 us -> none  [local(): group_pairs = lax.all_gather(pair_list, 'cols', axis=0, tiled=True)]
    unnamed x5 -> x7, local copies, waits for them, and re-layouts: 3.34 us -> 4.44 us
where the time goes in v2:
time: 94.3 us; the launch traced here: 94.1 us
  Pallas kernels  89.1 us (94%)
  local copies, waits for them, and re-layouts  4.44 us (5%)
    pallas_call x1, Pallas kernels, local(): pl.pallas_call(functools.partial(kernel, count), out_shape=(jax.ShapeDtyp...  89.1 us
    unnamed x7, local copies, waits for them, and re-layouts  4.44 us

profile of v2, /device:TPU:0, one launch (start us, length us, event | category | flops | bytes accessed | tf_op | source)
XLA Modules:
  0.0 94.1 jit_solution(17198422121245634506)
XLA Ops:
  0.6 0.8 copy.5.pair_ref
  1.4 0.0 copy-start
  1.4 1.4 %copy-done = bf16[2048,384]{1,0:T(8,128)(2,1)S(1)} copy-done((bf16[2048,384]{1,0:T(8,128)(2,1)S(1)}, bf16[2048,384]{1,0:T(8,128)(2,1)}, u32[]{:S(2)}) %copy-start) | copy-done | bytes 1572888
  2.8 0.0 copy-start.1
  2.8 0.9 %copy-done.1 = bf16[2048,64]{0,1:T(8,128)(2,1)S(1)} copy-done((bf16[2048,64]{0,1:T(8,128)(2,1)S(1)}, bf16[2048,64]{0,1:T(8,128)(2,1)}, u32[]{:S(2)}) %copy-start.1) | copy-done | bytes 262168
  3.8 89.1 %shard_map.50 = (f32[64,1024]{1,0:T(8,128)S(1)}, f32[64,64]{1,0:T(8,128)S(1)}) custom-call(s32[4,2]{1,0:T(4,128)S(1)} %copy.5.pair_ref, bf16[2048,384]{1,0:T(8,128)(2,1)S(1)} %copy-done, bf16[64,2048]{1,0:T(8,128)(2,1)S(1)} %bitcast.3), custom_call_target="tpu_custom_call" | custom-call | tf_op jit(solution)/shard_map/pallas_call | solution.py:506
  92.8 0.7 copy.8
  93.5 0.6 copy.9
Async XLA Ops:
  1.4 1.4 %copy-start = (bf16[2048,384]{1,0:T(8,128)(2,1)S(1)}, bf16[2048,384]{1,0:T(8,128)(2,1)}, u32[]{:S(2)}) copy-start(bf16[2048,384]{1,0:T(8,128)(2,1)} %emb_ref.1) | copy-start | bytes 4718596
  2.8 0.9 %copy-start.1 = (bf16[2048,64]{0,1:T(8,128)(2,1)S(1)}, bf16[2048,64]{0,1:T(8,128)(2,1)}, u32[]{:S(2)}) copy-start(bf16[2048,64]{0,1:T(8,128)(2,1)} %param.4) | copy-start | bytes 786436

commit v3 on v2

--- a/solution.py
+++ b/solution.py
@@ -91,11 +91,14 @@
     mir,
     sib_out,
     sib_in,
+    msib_out,
+    msib_in,
     mir_out,
     mir_in,
     gram_out,
     gram_in,
     load_sem,
+    test_sem,
     pair_sem,
     unit_send,
     unit_recv,
@@ -105,6 +108,8 @@
     vec_recv,
     sib_send,
     sib_recv,
+    msib_send,
+    msib_recv,
     mir_send,
     mir_recv,
     gram_send,
@@ -147,6 +152,14 @@
         for q in range(PIECES):
             load(side, q).start()
 
+    def test_load(b, n, place):
+        source = test_ref.at[:, pl.ds(b * BLK, BLK)]
+        return pltpu.make_async_copy(source, place.at[b], test_sem.at[b, n])
+
+    for b in (0, 1):
+        for n, place in enumerate((vown_0, vwin_0)):
+            test_load(b, n, place).start()
+
     barrier = pltpu.get_barrier_semaphore()
 
     def greet(device):
@@ -179,11 +192,10 @@
         own[block, pl.ds(q * PIECE, PIECE), :] = rows
         win[q][block] = rows
 
+    normalise(0, 0)
     for b in (0, 1):
-        block = test_ref[:, b * BLK : (b + 1) * BLK]
-        vown[0][b] = block
-        vwin[0][b] = block
-    normalise(0, 0)
+        for n, place in enumerate((vown_0, vwin_0)):
+            test_load(b, n, place).wait()
     pl.semaphore_wait(barrier, peers)
 
     pair_copy = remote(pair_ref, pair_in, pair_sem.at[0], pair_sem.at[1], (r, other))
@@ -317,6 +329,72 @@
     def forward(p, s, q, tile):
         return dot_nt(vwin[p][seconds[s], :, pl.ds(q * PIECE, PIECE)], tile)
 
+    def weight(flag):
+        return flag.astype(F32)
+
+    def mirror_sum(block, span):
+        total = None
+        for s in (0, 1):
+            off = jnp.logical_and(lives[s], firsts[s] != seconds[s])
+            term = weight(jnp.logical_and(off, seconds[s] == block)) * mir[s, :, span]
+            total = term if total is None else total + term
+        return total
+
+    def own_sum(block):
+        total = mirror_sum(block, slice(None))
+        for s in (0, 1):
+            total = total + weight(jnp.logical_and(lives[s], firsts[s] == block)) * fwd[s]
+        return total
+
+    def msib_copy(p, k, q):
+        return remote(
+            msib_out.at[p, k - 1, q], msib_in.at[p, k - 1, q],
+            msib_send.at[p, k - 1, q], msib_recv.at[p, k - 1, q], (r, other),
+        )
+
+    def mir_copy(p, k, q, device):
+        return remote(
+            mir_out.at[p, k - 1, q], mir_in.at[p, k - 1, q],
+            mir_send.at[p, k - 1, q], mir_recv.at[p, k - 1, q], device,
+        )
+
+    def share_mirror(p, q):
+        for k in (2, 1):
+            msib_out[p, k - 1, q] = mirror_sum(2 * k + other, pl.ds(q * PIECE, PIECE))
+            msib_copy(p, k, q).start()
+
+    def send_mirror(p, q):
+        for k in (2, 1):
+            mine = mirror_sum(2 * k + c, pl.ds(q * PIECE, PIECE))
+            msib_copy(p, k, q).wait_recv()
+            mir_out[p, k - 1, q] = (mine + msib_in[p, k - 1, q]).astype(BF16)
+
+            @pl.when(r + k < count)
+            def _(k=k):
+                mir_copy(p, k, q, (r + k, c)).start()
+
+    def sib_copy(p):
+        return remote(sib_out.at[p], sib_in.at[p], sib_send.at[p], sib_recv.at[p], (r, other))
+
+    def collect(p):
+        sib_out[p] = own_sum(other)
+        sib_copy(p).start()
+        total = own_sum(c)
+        sib_copy(p).wait_recv()
+        total = total + sib_in[p]
+        for q in range(PIECES):
+            for k in (1, 2):
+                @pl.when(r >= k)
+                def _(k=k, q=q):
+                    mir_copy(p, k, q, (r, other)).wait_recv()
+        parts = []
+        for q in range(PIECES):
+            part = total[:, q * PIECE : (q + 1) * PIECE]
+            for k in (1, 2):
+                part = part + mir_in[p, k - 1, q].astype(F32)
+            parts.append(part)
+        return jnp.concatenate(parts, axis=1)
+
     for q in range(PIECES):
         for h in range(SUBS):
             @pl.when(r + 2 < count)
@@ -335,6 +413,8 @@
                 unit_pass(1, q, h).start()
         if q == 0:
             vec_finish(0)
+        else:
+            send_mirror(0, q - 1)
         for h in range(SUBS):
             for k in (1, 2):
                 @pl.when(r + k < count)
@@ -345,60 +425,8 @@
             mirror(0, s, q, tile)
             term = forward(0, s, q, tile)
             fwd[s] = fwd[s] + term if q else term
-
-    def weight(flag):
-        return flag.astype(F32)
-
-    def block_sum(k, side):
-        total = None
-        for s in (0, 1):
-            here = 2 * k + side
-            off = jnp.logical_and(lives[s], firsts[s] != seconds[s])
-            term = weight(jnp.logical_and(off, seconds[s] == here)) * mir[s]
-            if k == 0:
-                term = term + weight(jnp.logical_and(lives[s], firsts[s] == here)) * fwd[s]
-            total = term if total is None else total + term
-        return total
-
-    def sib_copy(p, k):
-        return remote(
-            sib_out.at[k], sib_in.at[p, k], sib_send.at[p, k], sib_recv.at[p, k], (r, other)
-        )
-
-    def mir_copy(p, k, device):
-        return remote(
-            mir_out.at[p, k - 1], mir_in.at[p, k - 1],
-            mir_send.at[p, k - 1], mir_recv.at[p, k - 1], device,
-        )
-
-    def send_mirrors(p):
-        for k in (2, 1):
-            sib_out[k] = block_sum(k, other)
-            sib_copy(p, k).start()
-        for k in (2, 1):
-            mine = block_sum(k, c)
-            sib_copy(p, k).wait_recv()
-            mir_out[p, k - 1] = (mine + sib_in[p, k]).astype(BF16)
-
-            @pl.when(r + k < count)
-            def _(k=k):
-                mir_copy(p, k, (r + k, c)).start()
-
-    def collect(p):
-        sib_out[0] = block_sum(0, other)
-        sib_copy(p, 0).start()
-        total = block_sum(0, c)
-        sib_copy(p, 0).wait_recv()
-        total = total + sib_in[p, 0]
-        for k in (1, 2):
-            @pl.when(r >= k)
-            def _(k=k):
-                mir_copy(p, k, (r, other)).wait_recv()
-        for k in (1, 2):
-            total = total + mir_in[p, k - 1].astype(F32)
-        for k in (0, 1, 2):
-            sib_copy(p, k).wait_send()
-        return total
+        share_mirror(0, q)
+    send_mirror(0, PIECES - 1)
 
     def gram_copy(p, n, d, to, at_slot):
         return remote(
@@ -431,14 +459,16 @@
 
     def orthonormal(p, total):
         gram = dot_nt(total, total, lax.Precision.HIGHEST)
-        gram = sum_over_devices(p, gram) * (1.0 / rows_total)
+        half = gram.shape[0] // 2
+        packed = jnp.concatenate([gram[:half], gram[half:]], axis=1)
+        packed = sum_over_devices(p, packed) * (1.0 / rows_total)
+        gram = jnp.concatenate([packed[:, : 2 * half], packed[:, 2 * half :]], axis=0)
         upper, inverse = factor_and_inverse(gram)
         solved = jnp.dot(
             inverse, total, precision=lax.Precision.HIGHEST, preferred_element_type=F32
         )
         return solved, upper
 
-    send_mirrors(0)
     panel, _ = orthonormal(0, collect(0))
     panel = panel.astype(BF16)
     vown[1][c] = panel
@@ -446,10 +476,13 @@
     vec_start(1)
     vwin[1][c] = panel
     panel_copy(other).wait_recv()
-    for s in (0, 1):
-        for q in range(PIECES):
+    for q in range(PIECES):
+        for s in (0, 1):
             mirror(1, s, q, aff[s, q])
-    send_mirrors(1)
+        share_mirror(1, q)
+        if q:
+            send_mirror(1, q - 1)
+    send_mirror(1, PIECES - 1)
     vwin[1][other] = vown[1][other]
     vec_finish(1)
     for s in (0, 1):
@@ -462,6 +495,11 @@
     basis_ref[...] = basis
 
     panel_copy(c).wait_send()
+    for p in (0, 1):
+        sib_copy(p).wait_send()
+        for k in (1, 2):
+            for q in range(PIECES):
+                msib_copy(p, k, q).wait_send()
     for k in (1, 2):
         @pl.when(r >= k)
         def _(k=k):
@@ -472,7 +510,8 @@
         def _(k=k):
             for p in (0, 1):
                 vec_pass(p, k).wait_send()
-                mir_copy(p, k, (r + k, c)).wait_send()
+                for q in range(PIECES):
+                    mir_copy(p, k, q, (r + k, c)).wait_send()
             for q in range(PIECES):
                 for h in range(SUBS):
                     unit_pass(k, q, h).wait_send()
@@ -502,6 +541,7 @@
         stride *= min(QUAD, count // stride)
         steps += 1
     vmem = pl.BlockSpec(memory_space=pltpu.VMEM)
+    hbm = pl.BlockSpec(memory_space=pltpu.HBM)
     dma = pltpu.SemaphoreType.DMA
     basis, upper = pl.pallas_call(
         functools.partial(kernel, count),
@@ -509,7 +549,7 @@
             jax.ShapeDtypeStruct((columns, BLK), F32),
             jax.ShapeDtypeStruct((columns, columns), F32),
         ),
-        in_specs=[pl.BlockSpec(memory_space=pltpu.SMEM), pl.BlockSpec(memory_space=pl.ANY), vmem],
+        in_specs=[pl.BlockSpec(memory_space=pltpu.SMEM), hbm, hbm],
         out_specs=(vmem, vmem),
         scratch_shapes=[
             pltpu.VMEM((blocks * BLK, width), BF16),
@@ -521,13 +561,16 @@
             pltpu.VMEM((2, PIECES, BLK, PIECE), BF16),
             pltpu.VMEM((2, columns, BLK), F32),
             pltpu.VMEM((2, columns, BLK), F32),
-            pltpu.VMEM((3, columns, BLK), F32),
-            pltpu.VMEM((2, 3, columns, BLK), F32),
-            pltpu.VMEM((2, 2, columns, BLK), BF16),
-            pltpu.VMEM((2, 2, columns, BLK), BF16),
-            pltpu.VMEM((2, steps, columns, columns), F32),
-            pltpu.VMEM((2, steps, 2 * QUAD, columns, columns), F32),
+            pltpu.VMEM((2, columns, BLK), F32),
+            pltpu.VMEM((2, columns, BLK), F32),
+            pltpu.VMEM((2, 2, PIECES, columns, PIECE), F32),
+            pltpu.VMEM((2, 2, PIECES, columns, PIECE), F32),
+            pltpu.VMEM((2, 2, PIECES, columns, PIECE), BF16),
+            pltpu.VMEM((2, 2, PIECES, columns, PIECE), BF16),
+            pltpu.VMEM((2, steps, columns // 2, 2 * columns), F32),
+            pltpu.VMEM((2, steps, 2 * QUAD, columns // 2, 2 * columns), F32),
             dma((2, PIECES)),
+            dma((2, 2)),
             dma((2,)),
             dma((2, PIECES * SUBS)),
             dma((2, PIECES * SUBS)),
@@ -535,15 +578,17 @@
             dma((2, PIECES * SUBS)),
             dma((2, 5)),
             dma((2, 5)),
-            dma((2, 3)),
-            dma((2, 3)),
-            dma((2, 2)),
-            dma((2, 2)),
+            dma((2,)),
+            dma((2,)),
+            dma((2, 2, PIECES)),
+            dma((2, 2, PIECES)),
+            dma((2, 2, PIECES)),
+            dma((2, 2, PIECES)),
             dma((2, steps, 2 * QUAD)),
             dma((2, steps, 2 * QUAD)),
         ],
         compiler_params=pltpu.CompilerParams(
-            collective_id=0, has_side_effects=True, vmem_limit_bytes=48 * 1024 * 1024
+            collective_id=0, has_side_effects=True, vmem_limit_bytes=63 * 1024 * 1024
         ),
     )(pair_list, embeddings, test_matrix.T)
     return basis.T, upper

time: 94.3 us -> 87.5 us (0.928)
  Pallas kernels: 89.1 us -> 82.2 us
    pallas_call x1, Pallas kernels: 89.1 us -> 82.2 us  [local(): pl.pallas_call(functools.partial(kernel, count), out_shape=(jax.ShapeDtyp...]
    unnamed x7 -> x3, local copies, waits for them, and re-layouts: 4.44 us -> 4.38 us
where the time goes in v3:
time: 87.5 us; the launch traced here: 87.3 us
  Pallas kernels  82.2 us (94%)
  local copies, waits for them, and re-layouts  4.38 us (5%)
    pallas_call x1, Pallas kernels, local(): pl.pallas_call(functools.partial(kernel, count), out_shape=(jax.ShapeDtyp...  82.2 us
    unnamed x3, local copies, waits for them, and re-layouts  4.38 us

profile of v3, /device:TPU:0, one launch (start us, length us, event | category | flops | bytes accessed | tf_op | source)
XLA Modules:
  0.0 87.3 jit_solution(14021039544499822650)
XLA Ops:
  0.6 1.3 %copy.5.pair_ref = s32[4,2]{1,0:T(4,128)} copy(s32[4,2]{0,1:T(2,128)} %param.5) | data formatting | bytes 64 | tf_op args[2]
  2.0 82.2 %shard_map.50 = (f32[64,1024]{1,0:T(8,128)}, f32[64,64]{1,0:T(8,128)}) custom-call(s32[4,2]{1,0:T(4,128)} %copy.5.pair_ref, bf16[2048,384]{1,0:T(8,128)(2,1)} %emb_ref.1, bf16[64,2048]{1,0:T(8,128)(2,1)} %bitcast.3), custom_call_target="tpu_custom_call" | custom-call | tf_op jit(solution)/shard_map/pallas_call | solution.py:546
  84.2 1.7 %copy.8 = f32[1024,64]{0,1:T(8,128)} copy(f32[1024,64]{0,1:T(8,128)} %bitcast.2) | data formatting | bytes 524288
  85.9 1.4 %copy.9 = f32[64,64]{1,0:T(8,128)} copy(f32[64,64]{1,0:T(8,128)} %get-tuple-element.9) | data formatting | bytes 32768
